TPU v7x, 32 devices: a whole 2x2x4 slice. The times are simulated.
32 devices in a mesh: groups: 2 (over x), dp: 16 (over z, y, core).
Axes of the slice: x: 2, y: 2, z: 4, core: 2. Of those that a mesh axis runs over, the one named last changes fastest.
Arguments:
- features: bfloat16 [16384, 4096], P(('groups', 'dp')), parts along dimension 0, may hold values from -6 to 6
- upstream: bfloat16 [16384, 512], P(('groups', 'dp')), parts along dimension 0, may hold values from -0.29882812 to 0.29882812
- frozen_value: bfloat16 [4096, 512], replicated, may hold values from -0.25 to 0.25
- adapter_down: bfloat16 [24, 32, 4096], P('groups'), parts along dimension 0, may hold values from -0.09375 to 0.09375
- adapter_up: bfloat16 [24, 32, 512], P('groups'), parts along dimension 0, may hold values from -0.25 to 0.25
- block_adapter: int32 [128, 1], P(('groups', 'dp')), parts along dimension 0, may hold values from 0 to 11
- block_count: int32 [128], P(('groups', 'dp')), parts along dimension 0, may hold values from 1 to 128, as said below
Outputs:
- input_grad: bfloat16 [16384, 4096], P(('groups', 'dp')), parts along dimension 0
- grad_down: float32 [24, 32, 4096], P('groups', None, 'dp'), parts along dimension 0
- grad_up: float32 [24, 32, 512], P('groups', None, 'dp'), parts along dimension 0
There are 2 independent parts, one for each index of `groups`. A program takes and returns all parts, laid end to end along the dimension named above; an argument that names none is the same for every part. Nothing has to cross between parts.
Inputs may be any that keep to these rules, and one draw needn't show every extreme that they name: `block_adapter`: every adapter of 0 to 11 owns some block. Rows 0 to block_count - 1 of a block are live, the rest padding; some block is full and some has one live row.
All inputs are finite; a program needn't handle non-finite values.
Results may differ from a plain program's by a relative error of at most 0.0029.
Values may be sent and summed in bfloat16 or wider, within the bound.
A program may use at most 192 MiB of HBM per device.

v0:
```python
import jax
import jax.numpy as jnp
from jax import lax
from jax.sharding import PartitionSpec as P


def per_device(
    features, upstream, frozen_value, adapter_down, adapter_up, block_adapter, block_count
):
    nblk = block_count.shape[0]
    rows = features.shape[0] // nblk
    width = features.shape[1]
    outs = upstream.shape[1]
    tenants = adapter_down.shape[0]
    ids = block_adapter[:, 0]
    xblk = features.reshape(nblk, rows, width)
    yblk = upstream.reshape(nblk, rows, outs)
    down_sel = adapter_down[ids]
    up_sel = adapter_up[ids]
    position = lax.broadcasted_iota(jnp.int32, (nblk, rows), 1)
    live = (position < block_count[:, None]).astype(jnp.bfloat16)[:, None, :]
    low = (
        jnp.einsum("brd,bjd->brj", down_sel, xblk, preferred_element_type=jnp.float32).astype(
            jnp.bfloat16
        )
        * live
    )
    back = (
        jnp.einsum("bro,bjo->brj", up_sel, yblk, preferred_element_type=jnp.float32).astype(
            jnp.bfloat16
        )
        * live
    )
    frozen_term = jnp.einsum(
        "to,do->td", upstream, frozen_value, preferred_element_type=jnp.float32
    )
    adapter_term = jnp.einsum("brj,brd->bjd", back, down_sel, preferred_element_type=jnp.float32)
    live_rows = live[:, 0, :].reshape(nblk * rows, 1).astype(jnp.float32)
    input_grad = (
        live_rows * (frozen_term + 2.0 * adapter_term.reshape(nblk * rows, width))
    ).astype(jnp.bfloat16)
    tenant_ids = jnp.arange(tenants, dtype=jnp.int32)
    part_down = jnp.einsum("brj,bjd->brd", back, xblk, preferred_element_type=jnp.float32)
    part_up = jnp.einsum("brj,bjo->bro", low, yblk, preferred_element_type=jnp.float32)
    onehot = (ids[:, None] == tenant_ids[None, :]).astype(jnp.float32)
    dense_down = 2.0 * jnp.einsum("ba,brd->ard", onehot, part_down, precision=lax.Precision.HIGHEST)
    dense_up = 2.0 * jnp.einsum("ba,bro->aro", onehot, part_up, precision=lax.Precision.HIGHEST)
    grad_down, grad_up = (
        lax.psum_scatter(dense_down, "dp", scatter_dimension=2, tiled=True),
        lax.psum_scatter(dense_up, "dp", scatter_dimension=2, tiled=True),
    )
    return (input_grad, grad_down, grad_up)


def solution(mesh):
    return jax.shard_map(
        per_device,
        mesh=mesh,
        in_specs=(
            P(("groups", "dp"), None),
            P(("groups", "dp"), None),
            P(),
            P("groups", None, None),
            P("groups", None, None),
            P(("groups", "dp"), None),
            P(("groups", "dp")),
        ),
        out_specs=(P(("groups", "dp"), None), P("groups", None, "dp"), P("groups", None, "dp")),
        check_vma=False,
    )
```

profile of v0, /device:TPU:0, one launch (start us, length us, event | category | flops | bytes accessed | tf_op | source)
XLA Modules:
  0.0 210.5 jit_solution(2597756767369677964)
XLA Ops:
  7.2 0.0 copy-start
  7.2 0.0 copy-start.3
  7.2 0.0 reduce-scatter.7.cloned.1.call-start
  7.2 0.8 fusion.14
  8.0 0.8 bitcast_convert_fusion
  8.9 0.2 copy-done
  9.1 1.6 gather_fusion.1
  10.7 4.3 %fusion.5 = f32[4,32,512]{2,1,0:T(8,128)S(1)} fusion(bf16[4,128,512]{2,1,0:T(8,128)(2,1)} %bitcast.35, bf16[4,32,4096]{2,1,0:T(8,128)(2,1)} %gather_fusion.1, bf16[4,128,4096]{2,1,0:T(8,128)(2,1)} %bitcast.33, bf16[4,128]{1,0:T(4,128)(2,1)S(1)} %get-tuple-element.10), kind=kOutput, calls=%fused_computation.13 | convolution fusion | flops 151027712 | bytes 6030336 | tf_op jit(solution)/shard_map/brj,bjo->bro/dot_general | solution.py:44
  14.9 0.0 copy-done.3
  14.9 1.8 convolution_multiply_fusion.2
  16.8 8.5 %copy.16 = f32[12,32,512]{0,1,2:T(8,128)} copy(f32[12,32,512]{2,0,1:T(8,128)} %convolution_multiply_fusion.2) | data formatting | bytes 1572864
  25.2 8.5 %reshape.71 = f32[512,384]{1,0:T(8,128)} reshape(f32[512,32,12]{2,1,0:T(8,128)} %bitcast.32) | data formatting | bytes 1572864
  33.8 0.0 reduce-scatter.7.cloned.1.call-update
  33.8 0.2 reduce-scatter.5.cloned.1.call-start
  34.0 1.6 gather_fusion
  35.6 1.3 fusion.3
  36.9 2.9 %fusion.15 = f32[4,32,4096]{2,1,0:T(8,128)S(1)} fusion(bf16[4,32,128]{2,1,0:T(8,128)(2,1)S(1)} %fusion.3, bf16[4,128,4096]{2,1,0:T(8,128)(2,1)} %bitcast.34), kind=kOutput, calls=%fused_computation.26 | convolution fusion | flops 134217728 | bytes 6324224 | tf_op jit(solution)/shard_map/brj,bjd->brd/dot_general | solution.py:43
  39.8 7.1 %convolution_multiply_fusion = f32[12,32,4096]{2,0,1:T(8,128)} fusion(f32[4,32,4096]{2,1,0:T(8,128)S(1)} %fusion.15, s32[4]{0:T(128)S(1)} %bitcast.39), kind=kOutput, calls=%fused_computation.5 | convolution fusion | flops 77070384 | bytes 8388624 | tf_op jit(solution)/shard_map/ba,brd->ard/dot_general | solution.py:46
  46.9 0.0 reduce-scatter.5.cloned.1.call-update
  46.9 0.0 copy-start.1
  46.9 0.0 copy-start.2
  46.9 2.7 %convolution_multiply_fusion.1 = f32[4,128,4096]{2,1,0:T(8,128)S(1)} fusion(bf16[4,32,128]{2,1,0:T(8,128)(2,1)S(1)} %fusion.3, bf16[4,32,4096]{2,1,0:T(8,128)(2,1)} %gather_fusion.1), kind=kOutput, calls=%fused_computation.6 | convolution fusion | flops 136314880 | bytes 9469952 | tf_op jit(solution)/shard_map/brj,brd->bjd/dot_general | solution.py:37
  49.6 0.0 copy-done.1
  49.6 0.0 copy-done.2
  49.7 4.4 %fusion.1 = bf16[512,4096]{1,0:T(8,128)(2,1)} fusion(f32[4,128,4096]{2,1,0:T(8,128)S(1)} %convolution_multiply_fusion.1, bf16[512,512]{1,0:T(8,128)(2,1)S(1)} %copy-done.1, bf16[4096,512]{1,0:T(8,128)(2,1)S(1)} %copy-done.2, f32[512]{0:T(512)S(1)} %get-tuple-element.9), kind=kOutput, calls=%fused_computation.4 | convolution fusion | flops 2153775104 | bytes 17303552 | tf_op jit(solution)/shard_map/to,do->td/dot_general | solution.py:34
  54.1 39.2 %reduce-scatter.7.cloned.1.call-done = f32[32,384]{1,0:T(8,128)} async-done(((f32[512,384]{1,0:T(8,128)}), f32[32,384]{1,0:T(8,128)}) %reduce-scatter.7.cloned.1.call-update) | async-done | bytes 49168
  93.2 2.2 %reshape.72 = f32[32,32,12]{2,1,0:T(8,128)} reshape(f32[32,384]{1,0:T(8,128)} %reduce-scatter.7.cloned.1.call-done) | data formatting | bytes 98304
  95.4 2.1 copy.13
  97.5 104.2 %reduce-scatter.5.cloned.1.call-done = f32[12,32,256]{2,0,1:T(8,128)} async-done(((f32[12,32,4096]{2,0,1:T(8,128)}), f32[12,32,256]{2,0,1:T(8,128)}) %reduce-scatter.5.cloned.1.call-update) | async-done | bytes 393232 | tf_op jit(solution)/shard_map/reduce_scatter | solution.py:49
  201.7 2.0 copy.12
  (1 shorter events, 0.0 us)
Async XLA Ops:
  7.2 1.9 copy-start
  7.2 7.7 %copy-start.3 = (s32[4,1]{0,1:T(1,128)S(1)}, s32[4,1]{0,1:T(1,128)}, u32[]{:S(2)}) copy-start(s32[4,1]{0,1:T(1,128)} %param.12) | copy-start | bytes 52
  7.2 86.1 %reduce-scatter.7.cloned.1.call-start = ((), (), s32[]{:S(2)}) async-start(), calls=%async_computation.3 | async-start | bytes 835584
  33.8 167.9 %reduce-scatter.5.cloned.1.call-start = ((), (), s32[]{:S(2)}) async-start(), calls=%async_computation.2 | async-start | bytes 8912896 | tf_op jit(solution)/shard_map/reduce_scatter | solution.py:49
  46.9 2.7 %copy-start.1 = (bf16[512,512]{1,0:T(8,128)(2,1)S(1)}, bf16[512,512]{1,0:T(8,128)(2,1)}, u32[]{:S(2)}) copy-start(bf16[512,512]{1,0:T(8,128)(2,1)} %param.8) | copy-start | bytes 1572868
  46.9 2.7 %copy-start.2 = (bf16[4096,512]{1,0:T(8,128)(2,1)S(1)}, bf16[4096,512]{1,0:T(8,128)(2,1)}, u32[]{:S(2)}) copy-start(bf16[4096,512]{1,0:T(8,128)(2,1)} %param.9) | copy-start | bytes 12582916
Sparse Core Ops, SparseCore 0:
  33.9 59.2 reduce-scatter.6
  97.9 103.7 reduce-scatter.4
where the time goes:
time: 211 us
  waiting for transfers between devices  143 us (68%)
  local copies, waits for them, and re-layouts  26.7 us (13%)
  matrix products  24.5 us (12%)
  between operations  14.1 us (7%)
    reduce_scatter x1, waiting for transfers between devices, per_device(): lax.psum_scatter(dense_down, 'dp', scatter_dimension=2, tiled=True)  104 us
    unnamed x3, waiting for transfers between devices  39.2 us
    unnamed x13, local copies, waits for them, and re-layouts  23.6 us
    dot_general x1, matrix products, per_device(): jnp.einsum('ba,brd->ard', onehot, part_down, precision=lax.Precision.HIGH...  7.1 us
    dot_general x1, matrix products, per_device(): jnp.einsum('to,do->td', upstream, frozen_value, preferred_element_type=jn...  4.42 us
    dot_general x1, matrix products, per_device(): jnp.einsum('brj,bjo->bro', low, yblk, preferred_element_type=jnp.float32)  4.26 us
  transfers between devices with their start and end apart: 2, of which 2 were waited for; matrix products, arithmetic and copies ran while one was open for 11% of the time, Pallas kernels for 0%

commit v1 on v0

v1 whole, which is shorter than its diff:
```python
import functools

import jax
import jax.numpy as jnp
from jax import lax
from jax.experimental import pallas as pl
from jax.experimental.pallas import tpu as pltpu
from jax.sharding import PartitionSpec as P

MESH = pl.DeviceIdType.MESH
BF, F32, I32 = jnp.bfloat16, jnp.float32, jnp.int32
INNER = 4
TILE = 512


def dot_nt(a, b):
    return lax.dot_general(a, b, (((1,), (1,)), ((), ())), preferred_element_type=F32)


def dot_nn(a, b):
    return jnp.dot(a, b, preferred_element_type=F32)


def iota(shape, dim):
    return lax.broadcasted_iota(I32, shape, dim)


def chunk_order(outer):
    rows = []
    for z in range(outer):
        row = []
        for t in range(outer - 1):
            if t >= z:
                row.append(z + outer - 1 - t)
            if t >= outer - 1 - z:
                row.append(t - (outer - 1 - z))
        rows.append(row + [z])
    return rows


def kernel(
    dims,
    ids_ref,
    cnt_ref,
    x_hbm,
    y_hbm,
    fz_hbm,
    dn_hbm,
    up_hbm,
    gin_hbm,
    gdn_ref,
    gup_ref,
    x_v,
    y_v,
    fz_v,
    dn_v,
    up_v,
    dsel,
    ylive,
    back2,
    o_v,
    idm,
    idr,
    msg,
    rmsg,
    umsg,
    rumsg,
    e_down,
    e_up,
    acc,
    uacc,
    ls,
    lr,
    lus,
    lur,
    ld_sem,
    x_sem,
    o_sem,
    id_ss,
    id_rs,
    m_ss,
    m_rs,
    u_ss,
    u_rs,
    l_ss,
    l_rs,
    lu_ss,
    lu_rs,
):
    nblk, rows, rank, tenants, outer, w, oc = dims
    tokens, width = x_v.shape
    outs = y_v.shape[1]
    br = nblk * rank
    slab = INNER * w
    me = lax.axis_index("dp")
    z = me // INNER
    mi = me % INNER
    group = lax.axis_index("groups")

    def dev(d):
        return (group, d)

    loads = [
        pltpu.make_async_copy(y_hbm, y_v, ld_sem.at[0]),
        pltpu.make_async_copy(up_hbm, up_v, ld_sem.at[1]),
        pltpu.make_async_copy(dn_hbm, dn_v, ld_sem.at[2]),
        pltpu.make_async_copy(fz_hbm, fz_v, ld_sem.at[3]),
    ]
    loads[0].start()
    loads[1].start()
    table = chunk_order(outer)
    order = []
    for k in range(outer):
        zk = jnp.int32(0)
        for place in range(outer):
            zk = jnp.where(z == place, table[place][k], zk)
        order.append(zk)

    def slab_of(zc):
        return pl.ds(pl.multiple_of(zc * slab, slab), slab)

    def x_load(zc):
        return pltpu.make_async_copy(x_hbm.at[:, slab_of(zc)], x_v.at[:, slab_of(zc)], x_sem.at[zc])

    for k in range(outer):
        x_load(order[k]).start()
    loads[2].start()
    loads[3].start()

    barrier = pltpu.get_barrier_semaphore()
    for k in range(1, INNER):
        pl.semaphore_signal(barrier, inc=1, device_id=dev(z * INNER + (mi + k) % INNER), device_id_type=MESH)

    @pl.when(z > 0)
    def _():
        pl.semaphore_signal(barrier, inc=1, device_id=dev(me - INNER), device_id_type=MESH)

    @pl.when(z < outer - 1)
    def _():
        pl.semaphore_signal(barrier, inc=1, device_id=dev(me + INNER), device_id_type=MESH)

    lanes = idm.shape[1]
    lane = iota((16, lanes), 1)
    half = iota((16, lanes), 0) < 8
    by_rank = jnp.zeros((16, lanes), F32)
    by_col = jnp.zeros((16, lanes), F32)
    row_id = jnp.zeros((br, 1), I32)
    row_cnt = jnp.zeros((br, 1), I32)
    lane_cnt = jnp.zeros((1, br), I32)
    tok_cnt = jnp.zeros((tokens, 1), I32)
    for b in range(nblk):
        a_b = ids_ref[b, 0]
        c_b = cnt_ref[b]
        by_rank = jnp.where(lane // rank == b, a_b.astype(F32), by_rank)
        by_col = jnp.where(lane // oc == b, a_b.astype(F32), by_col)
        row_id = jnp.where(iota((br, 1), 0) // rank == b, a_b, row_id)
        row_cnt = jnp.where(iota((br, 1), 0) // rank == b, c_b, row_cnt)
        lane_cnt = jnp.where(iota((1, br), 1) // rank == b, c_b, lane_cnt)
        tok_cnt = jnp.where(iota((tokens, 1), 0) // rows == b, c_b, tok_cnt)
    idm[...] = jnp.where(half, by_rank, by_col).astype(BF)
    idr[mi] = idm[...]

    pick_shape = (br, tenants * rank)
    pick = (
        jnp.where(
            (iota(pick_shape, 1) // rank == row_id)
            & (iota(pick_shape, 1) % rank == iota(pick_shape, 0) % rank),
            1.0,
            0.0,
        )
    ).astype(BF)
    shape_t = (br, tokens)
    mask_t = (iota(shape_t, 0) // rank == iota(shape_t, 1) // rows) & (iota(shape_t, 1) % rows < row_cnt)
    shape_n = (tokens, br)
    mask_n = (iota(shape_n, 1) // rank == iota(shape_n, 0) // rows) & (iota(shape_n, 0) % rows < lane_cnt)

    loads[0].wait()
    loads[1].wait()
    up_sel = dot_nn(pick, up_v[...]).astype(BF)
    back_t = jnp.where(mask_t, dot_nt(up_sel, y_v[...]).astype(BF).astype(F32), 0.0).astype(BF)

    def id_copy(k, src_of):
        peer = (mi + k) % INNER
        return pltpu.make_async_remote_copy(
            src_ref=idm,
            dst_ref=idr.at[src_of],
            send_sem=id_ss.at[peer],
            recv_sem=id_rs.at[src_of],
            device_id=dev(z * INNER + peer),
            device_id_type=MESH,
        )

    def m_copy(zc, k, src_of):
        peer = (mi + k) % INNER
        return pltpu.make_async_remote_copy(
            src_ref=msg.at[zc, peer],
            dst_ref=rmsg.at[zc, src_of],
            send_sem=m_ss.at[zc, peer],
            recv_sem=m_rs.at[zc, src_of],
            device_id=dev(z * INNER + peer),
            device_id_type=MESH,
        )

    def u_copy(zc, k, src_of):
        peer = (mi + k) % INNER
        return pltpu.make_async_remote_copy(
            src_ref=umsg.at[zc, peer],
            dst_ref=rumsg.at[zc, src_of],
            send_sem=u_ss.at[zc, peer],
            recv_sem=u_rs.at[zc, src_of],
            device_id=dev(z * INNER + peer),
            device_id_type=MESH,
        )

    def send_chunk(zc):
        x_load(zc).wait()
        part = (2.0 * dot_nn(back_t, x_v[:, slab_of(zc)])).astype(BF)
        for i in range(INNER):
            msg[zc, i] = part[:, i * w : (i + 1) * w]
        for k in range(1, INNER):
            m_copy(zc, k, mi).start()
        rmsg[zc, mi] = msg[zc, mi]

    one = jnp.int32(1)
    pl.semaphore_wait(
        barrier, INNER - 1 + jnp.where(z > 0, one, 0) + jnp.where(z < outer - 1, one, 0)
    )
    for k in range(1, INNER):
        id_copy(k, mi).start()
    send_chunk(order[0])

    loads[2].wait()

    def select_step(j, carry):
        cols = pl.ds(pl.multiple_of(j * TILE, TILE), TILE)
        dsel[:, cols] = dot_nn(pick, dn_v[:, cols]).astype(BF)
        return carry

    lax.fori_loop(0, width // TILE, select_step, 0)
    low_sum = dot_nt(dsel[:, slab_of(order[0])], x_v[:, slab_of(order[0])])
    for k in range(1, outer):
        send_chunk(order[k])
        low_sum = low_sum + dot_nt(dsel[:, slab_of(order[k])], x_v[:, slab_of(order[k])])
    low_t = jnp.where(mask_t, low_sum.astype(BF).astype(F32), 0.0).astype(BF)
    part_up = 2.0 * dot_nn(low_t, y_v[...])
    for zc in range(outer):
        for i in range(INNER):
            at = (zc * INNER + i) * oc
            umsg[zc, i] = jnp.concatenate(
                [part_up[b * rank : (b + 1) * rank, at : at + oc] for b in range(nblk)], axis=1
            ).astype(BF)
    for k in range(outer):
        for j in range(1, INNER):
            u_copy(order[k], j, mi).start()
    for zc in range(outer):
        rumsg[zc, mi] = umsg[zc, mi]

    ylive[...] = jnp.where(
        iota((tokens, 1), 0) % rows < tok_cnt, y_v[...].astype(F32), 0.0
    ).astype(BF)
    back2[...] = jnp.where(
        mask_n, 2.0 * dot_nt(y_v[...], up_sel).astype(BF).astype(F32), 0.0
    ).astype(BF)

    for k in range(1, INNER):
        id_copy(k, (mi + INNER - k) % INNER).wait_recv()
    e_shape = (tenants * rank, br)
    u_shape = (tenants * oc, nblk * oc)
    for i in range(INNER):
        got = idr[i].astype(F32)
        e_down[:, i * br : (i + 1) * br] = jnp.where(
            ((iota(e_shape, 0) // rank).astype(F32) == got[0:1, :br])
            & (iota(e_shape, 0) % rank == iota(e_shape, 1) % rank),
            1.0,
            0.0,
        ).astype(BF)
        e_up[i] = jnp.where(
            ((iota(u_shape, 0) // oc).astype(F32) == got[8:9, : nblk * oc])
            & (iota(u_shape, 0) % oc == iota(u_shape, 1) % oc),
            1.0,
            0.0,
        ).astype(BF)

    tiles = width // TILE
    loads[3].wait()

    def o_copy(j):
        cols = pl.ds(pl.multiple_of(j * TILE, TILE), TILE)
        return pltpu.make_async_copy(o_v.at[:, cols], gin_hbm.at[:, cols], o_sem.at[j])

    def grad_tile(j, carry):
        cols = pl.ds(pl.multiple_of(j * TILE, TILE), TILE)
        o_v[:, cols] = (
            dot_nt(ylive[...], fz_v[cols, :]) + dot_nn(back2[...], dsel[:, cols])
        ).astype(BF)
        o_copy(j).start()
        return carry

    def merged(zc):
        for k in range(1, INNER):
            m_copy(zc, k, (mi + INNER - k) % INNER).wait_recv()
        acc[...] = dot_nn(e_down[...], rmsg[zc].reshape(INNER * br, w))

    def umerged(zc):
        for k in range(1, INNER):
            u_copy(zc, k, (mi + INNER - k) % INNER).wait_recv()
        total = dot_nt(rumsg[zc, 0], e_up[0])
        for i in range(1, INNER):
            total = total + dot_nt(rumsg[zc, i], e_up[i])
        uacc[...] = total

    def line_copy(way, zc, up):
        src, dst = (lus, lur) if up else (ls, lr)
        ss, rs = (lu_ss, lu_rs) if up else (l_ss, l_rs)
        return pltpu.make_async_remote_copy(
            src_ref=src.at[way, zc],
            dst_ref=dst.at[way, zc],
            send_sem=ss.at[way, zc],
            recv_sem=rs.at[way, zc],
            device_id=dev(me + INNER if way == 0 else me - INNER),
            device_id_type=MESH,
        )

    def take(way, zc, up):
        line_copy(way, zc, up).wait_recv()
        if up:
            uacc[...] += lur[way, zc].astype(F32)
        else:
            acc[...] += lr[way, zc].astype(F32)

    def hop(way, zc):
        fed = z > 0 if way == 0 else z < outer - 1
        merged(zc)

        @pl.when(fed)
        def _():
            take(way, zc, False)

        ls[way, zc] = acc[...].astype(BF)
        line_copy(way, zc, False).start()
        umerged(zc)

        @pl.when(fed)
        def _():
            take(way, zc, True)

        lus[way, zc] = uacc[...].astype(BF)
        line_copy(way, zc, True).start()

    first = (2 * tiles) // (outer + 1)
    lax.fori_loop(0, first, grad_tile, 0)

    def line_step(t, carry):
        @pl.when(t >= z)
        def _():
            hop(0, z + outer - 1 - t)

        @pl.when(t >= outer - 1 - z)
        def _():
            hop(1, t - (outer - 1 - z))

        lo = first + (t * (tiles - first)) // (outer - 1)
        hi = first + ((t + 1) * (tiles - first)) // (outer - 1)
        lax.fori_loop(lo, hi, grad_tile, 0)
        return carry

    lax.fori_loop(0, outer - 1, line_step, 0)

    merged(z)
    umerged(z)

    @pl.when(z > 0)
    def _():
        take(0, z, False)
        take(0, z, True)

    @pl.when(z < outer - 1)
    def _():
        take(1, z, False)
        take(1, z, True)

    gdn_ref[...] = acc[...]
    gup_ref[...] = uacc[...]

    for k in range(1, INNER):
        id_copy(k, mi).wait_send()

    def drain(zc, carry):
        for k in range(1, INNER):
            m_copy(zc, k, mi).wait_send()
            u_copy(zc, k, mi).wait_send()

        @pl.when(zc > z)
        def _():
            line_copy(0, zc, False).wait_send()
            line_copy(0, zc, True).wait_send()

        @pl.when(zc < z)
        def _():
            line_copy(1, zc, False).wait_send()
            line_copy(1, zc, True).wait_send()

        return carry

    lax.fori_loop(0, outer, drain, 0)

    def drain_out(j, carry):
        o_copy(j).wait()
        return carry

    lax.fori_loop(0, tiles, drain_out, 0)


def per_device(
    features, upstream, frozen_value, adapter_down, adapter_up, block_adapter, block_count, *, n
):
    tokens, width = features.shape
    outs = upstream.shape[1]
    tenants, rank = adapter_down.shape[:2]
    nblk = block_count.shape[0]
    rows = tokens // nblk
    outer = n // INNER
    w, oc = width // n, outs // n
    br = nblk * rank
    lanes = max(br, nblk * oc)
    ar = tenants * rank
    dims = (nblk, rows, rank, tenants, outer, w, oc)
    V = pltpu.VMEM
    D = pltpu.SemaphoreType.DMA
    anyspec = pl.BlockSpec(memory_space=pl.ANY)
    smem = pl.BlockSpec(memory_space=pltpu.SMEM)
    vmem = pl.BlockSpec(memory_space=pltpu.VMEM)
    gin, gdn, gup = pl.pallas_call(
        functools.partial(kernel, dims),
        out_shape=(
            jax.ShapeDtypeStruct((tokens, width), BF),
            jax.ShapeDtypeStruct((ar, w), F32),
            jax.ShapeDtypeStruct((rank, tenants * oc), F32),
        ),
        in_specs=[smem, smem] + [anyspec] * 5,
        out_specs=(anyspec, vmem, vmem),
        scratch_shapes=[
            V((tokens, width), BF),
            V((tokens, outs), BF),
            V((width, outs), BF),
            V((ar, width), BF),
            V((ar, outs), BF),
            V((br, width), BF),
            V((tokens, outs), BF),
            V((tokens, br), BF),
            V((tokens, width), BF),
            V((16, lanes), BF),
            V((INNER, 16, lanes), BF),
            V((outer, INNER, br, w), BF),
            V((outer, INNER, br, w), BF),
            V((outer, INNER, rank, nblk * oc), BF),
            V((outer, INNER, rank, nblk * oc), BF),
            V((ar, INNER * br), BF),
            V((INNER, tenants * oc, nblk * oc), BF),
            V((ar, w), F32),
            V((rank, tenants * oc), F32),
            V((2, outer, ar, w), BF),
            V((2, outer, ar, w), BF),
            V((2, outer, rank, tenants * oc), BF),
            V((2, outer, rank, tenants * oc), BF),
            D((4,)),
            D((outer,)),
            D((width // TILE,)),
            D((INNER,)),
            D((INNER,)),
            D((outer, INNER)),
            D((outer, INNER)),
            D((outer, INNER)),
            D((outer, INNER)),
            D((2, outer)),
            D((2, outer)),
            D((2, outer)),
            D((2, outer)),
        ],
        compiler_params=pltpu.CompilerParams(
            collective_id=0, has_side_effects=True, vmem_limit_bytes=56 * 1024 * 1024
        ),
        cost_estimate=pl.CostEstimate(
            flops=2 * tokens * width * (outs + 3 * br),
            bytes_accessed=2 * (2 * tokens * width + width * outs + ar * width),
            transcendentals=0,
        ),
    )(
        block_adapter,
        block_count,
        features,
        upstream,
        frozen_value,
        adapter_down.reshape(ar, width),
        adapter_up.reshape(ar, outs),
    )
    grad_up = gup.reshape(rank, tenants, oc).transpose(1, 0, 2)
    return gin, gdn.reshape(tenants, rank, w), grad_up


def solution(mesh):
    return jax.shard_map(
        functools.partial(per_device, n=mesh.shape["dp"]),
        mesh=mesh,
        in_specs=(
            P(("groups", "dp"), None),
            P(("groups", "dp"), None),
            P(),
            P("groups", None, None),
            P("groups", None, None),
            P(("groups", "dp"), None),
            P(("groups", "dp")),
        ),
        out_specs=(P(("groups", "dp"), None), P("groups", None, "dp"), P("groups", None, "dp")),
        check_vma=False,
    )
```

time: 211 us -> 44.7 us (0.21)
  waiting for transfers between devices: 143 us -> 0 us
  Pallas kernels: 0 us -> 35.4 us
  matrix products: 24.5 us -> 0 us
  local copies, waits for them, and re-layouts: 26.7 us -> 8.45 us
  between operations: 14.1 us -> 0.65 us
    reduce_scatter x1 -> x0, waiting for transfers between devices: 104 us -> none  [per_device(): lax.psum_scatter(dense_down, 'dp', scatter_dimension=2, tiled=True)]
    unnamed x3 -> x0, waiting for transfers between devices: 39.2 us -> none
    pallas_call x0 -> x1, Pallas kernels: none -> 35.4 us  [per_device(): pl.pallas_call(functools.partial(kernel, dims), out_shape=(jax.ShapeDtype...]
    dot_general x7 -> x0, matrix products: 24.5 us -> none  [the longest x1 7.1 us: per_device(): jnp.einsum('ba,brd->ard', onehot, part_down, precision=lax.Precision.HIGH...]
    unnamed x13 -> x6, local copies, waits for them, and re-layouts: 23.6 us -> 7.55 us
    gather x2 -> x0, local copies, waits for them, and re-layouts: 3.13 us -> none  [the longest x1 1.58 us: per_device(): down_sel = adapter_down[ids]]
  transfers between devices with their start and end apart: 2 -> 0, of which waited for: 2 -> 0; matrix products, arithmetic and copies ran while one was open for 11% -> 0% of each run, Pallas kernels for 0% -> 0%
where the time goes in v1:
time: 44.7 us; the launch traced here: 44.5 us
  Pallas kernels  35.4 us (79%)
  local copies, waits for them, and re-layouts  8.45 us (19%)
  between operations  0.65 us (1%)
    pallas_call x1, Pallas kernels, per_device(): pl.pallas_call(functools.partial(kernel, dims), out_shape=(jax.ShapeDtype...  35.4 us
    unnamed x6, local copies, waits for them, and re-layouts  7.55 us
    reshape x1, local copies, waits for them, and re-layouts, per_device(): grad_up = gup.reshape(rank, tenants, oc).transpose(1, 0, 2)  0.9 us

profile of v1, /device:TPU:0, one launch (start us, length us, event | category | flops | bytes accessed | tf_op | source)
XLA Modules:
  0.0 44.5 jit_solution(1840689458881346655)
XLA Ops:
  0.6 1.3 %copy.12.ids_ref = s32[4,1]{1,0:T(4,128)} copy(s32[4,1]{0,1:T(1,128)} %param.12) | data formatting | bytes 32 | tf_op args[5]
  1.9 35.4 %shard_map.94 = (bf16[512,4096]{1,0:T(8,128)(2,1)}, f32[384,256]{1,0:T(8,128)}, f32[32,384]{1,0:T(8,128)}) custom-call(s32[4,1]{1,0:T(4,128)} %copy.12.ids_ref, s32[4]{0:T(128)} %cnt_ref.1, bf16[512,4096]{1,0:T(8,128)(2,1)} %x_hbm.1, bf16[512,512]{1,0:T(8,128)(2,1)} %y_hbm.1, bf16[4096,512]{1,0:T(8,128)(2,1)} %fz_hbm.1, bf16[384,4096]{1,0:T(8,128)(2,1)} %bitcast.6, ...), custom_call_target="tpu_custom_call" | custom-call | flops 3758096384 | bytes 15728640 | tf_op jit(solution)/shard_map/pallas_call | solution.py:433
  37.3 0.9 %reshape.21 = f32[32,12,32]{2,1,0:T(8,128)S(1)} reshape(f32[32,384]{1,0:T(8,128)} %get-tuple-element.8) | data formatting | bytes 98304 | tf_op jit(solution)/shard_map/reshape | solution.py:497
  38.2 0.7 %copy.13 = f32[12,32,32]{2,1,0:T(8,128)} copy(f32[12,32,32]{2,0,1:T(8,128)S(1)} %bitcast.4) | data formatting | bytes 98304
  39.0 0.0 copy-start
  39.0 4.7 %copy.16 = bf16[512,4096]{1,0:T(8,128)(2,1)} copy(bf16[512,4096]{1,0:T(8,128)(2,1)} %get-tuple-element.15) | data formatting | bytes 8388608
  43.7 0.0 copy-done
  43.7 0.7 %copy.17 = f32[12,32,256]{2,1,0:T(8,128)} copy(f32[12,32,256]{2,1,0:T(8,128)S(1)} %bitcast.5) | data formatting | bytes 786432
Async XLA Ops:
  39.0 4.8 %copy-start = (f32[384,256]{1,0:T(8,128)S(1)}, f32[384,256]{1,0:T(8,128)}, u32[]{:S(2)}) copy-start(f32[384,256]{1,0:T(8,128)} %get-tuple-element.7) | copy-start | bytes 1179652

commit v2 on v1

--- a/solution.py
+++ b/solution.py
@@ -47,7 +47,7 @@
     fz_hbm,
     dn_hbm,
     up_hbm,
-    gin_hbm,
+    o_v,
     gdn_ref,
     gup_ref,
     x_v,
@@ -58,7 +58,6 @@
     dsel,
     ylive,
     back2,
-    o_v,
     idm,
     idr,
     msg,
@@ -75,7 +74,6 @@
     lur,
     ld_sem,
     x_sem,
-    o_sem,
     id_ss,
     id_rs,
     m_ss,
@@ -149,7 +147,7 @@
     lane_cnt = jnp.zeros((1, br), I32)
     tok_cnt = jnp.zeros((tokens, 1), I32)
     for b in range(nblk):
-        a_b = ids_ref[b, 0]
+        a_b = ids_ref[b]
         c_b = cnt_ref[b]
         by_rank = jnp.where(lane // rank == b, a_b.astype(F32), by_rank)
         by_col = jnp.where(lane // oc == b, a_b.astype(F32), by_col)
@@ -213,7 +211,6 @@
         )
 
     def send_chunk(zc):
-        x_load(zc).wait()
         part = (2.0 * dot_nn(back_t, x_v[:, slab_of(zc)])).astype(BF)
         for i in range(INNER):
             msg[zc, i] = part[:, i * w : (i + 1) * w]
@@ -227,6 +224,7 @@
     )
     for k in range(1, INNER):
         id_copy(k, mi).start()
+    x_load(order[0]).wait()
     send_chunk(order[0])
 
     loads[2].wait()
@@ -237,11 +235,10 @@
         return carry
 
     lax.fori_loop(0, width // TILE, select_step, 0)
-    low_sum = dot_nt(dsel[:, slab_of(order[0])], x_v[:, slab_of(order[0])])
     for k in range(1, outer):
-        send_chunk(order[k])
-        low_sum = low_sum + dot_nt(dsel[:, slab_of(order[k])], x_v[:, slab_of(order[k])])
-    low_t = jnp.where(mask_t, low_sum.astype(BF).astype(F32), 0.0).astype(BF)
+        x_load(order[k]).wait()
+    low = dot_nt(x_v[...], dsel[...]).astype(BF).astype(F32)
+    low_t = jnp.where(mask_t, low.T, 0.0).astype(BF)
     part_up = 2.0 * dot_nn(low_t, y_v[...])
     for zc in range(outer):
         for i in range(INNER):
@@ -252,6 +249,7 @@
     for k in range(outer):
         for j in range(1, INNER):
             u_copy(order[k], j, mi).start()
+    send_chunk(order[1])
     for zc in range(outer):
         rumsg[zc, mi] = umsg[zc, mi]
 
@@ -284,16 +282,11 @@
     tiles = width // TILE
     loads[3].wait()
 
-    def o_copy(j):
-        cols = pl.ds(pl.multiple_of(j * TILE, TILE), TILE)
-        return pltpu.make_async_copy(o_v.at[:, cols], gin_hbm.at[:, cols], o_sem.at[j])
-
     def grad_tile(j, carry):
         cols = pl.ds(pl.multiple_of(j * TILE, TILE), TILE)
         o_v[:, cols] = (
             dot_nt(ylive[...], fz_v[cols, :]) + dot_nn(back2[...], dsel[:, cols])
         ).astype(BF)
-        o_copy(j).start()
         return carry
 
     def merged(zc):
@@ -347,7 +340,7 @@
         lus[way, zc] = uacc[...].astype(BF)
         line_copy(way, zc, True).start()
 
-    first = (2 * tiles) // (outer + 1)
+    first = 0
     lax.fori_loop(0, first, grad_tile, 0)
 
     def line_step(t, carry):
@@ -364,7 +357,10 @@
         lax.fori_loop(lo, hi, grad_tile, 0)
         return carry
 
-    lax.fori_loop(0, outer - 1, line_step, 0)
+    for t in range(outer - 1):
+        line_step(t, 0)
+        if t + 2 < outer:
+            send_chunk(order[t + 2])
 
     merged(z)
     umerged(z)
@@ -379,8 +375,9 @@
         take(1, z, False)
         take(1, z, True)
 
-    gdn_ref[...] = acc[...]
-    gup_ref[...] = uacc[...]
+    for a in range(tenants):
+        gdn_ref[a] = acc[a * rank : (a + 1) * rank, :]
+        gup_ref[a] = uacc[:, a * oc : (a + 1) * oc]
 
     for k in range(1, INNER):
         id_copy(k, mi).wait_send()
@@ -403,12 +400,6 @@
         return carry
 
     lax.fori_loop(0, outer, drain, 0)
-
-    def drain_out(j, carry):
-        o_copy(j).wait()
-        return carry
-
-    lax.fori_loop(0, tiles, drain_out, 0)
 
 
 def per_device(
@@ -433,12 +424,12 @@
     gin, gdn, gup = pl.pallas_call(
         functools.partial(kernel, dims),
         out_shape=(
-            jax.ShapeDtypeStruct((tokens, width), BF),
-            jax.ShapeDtypeStruct((ar, w), F32),
-            jax.ShapeDtypeStruct((rank, tenants * oc), F32),
+            pltpu.VMEM((tokens, width), BF),
+            jax.ShapeDtypeStruct((tenants, rank, w), F32),
+            jax.ShapeDtypeStruct((tenants, rank, oc), F32),
         ),
         in_specs=[smem, smem] + [anyspec] * 5,
-        out_specs=(anyspec, vmem, vmem),
+        out_specs=(vmem, vmem, vmem),
         scratch_shapes=[
             V((tokens, width), BF),
             V((tokens, outs), BF),
@@ -448,7 +439,6 @@
             V((br, width), BF),
             V((tokens, outs), BF),
             V((tokens, br), BF),
-            V((tokens, width), BF),
             V((16, lanes), BF),
             V((INNER, 16, lanes), BF),
             V((outer, INNER, br, w), BF),
@@ -465,7 +455,6 @@
             V((2, outer, rank, tenants * oc), BF),
             D((4,)),
             D((outer,)),
-            D((width // TILE,)),
             D((INNER,)),
             D((INNER,)),
             D((outer, INNER)),
@@ -478,7 +467,7 @@
             D((2, outer)),
         ],
         compiler_params=pltpu.CompilerParams(
-            collective_id=0, has_side_effects=True, vmem_limit_bytes=56 * 1024 * 1024
+            collective_id=0, has_side_effects=True, vmem_limit_bytes=58 * 1024 * 1024
         ),
         cost_estimate=pl.CostEstimate(
             flops=2 * tokens * width * (outs + 3 * br),
@@ -486,7 +475,7 @@
             transcendentals=0,
         ),
     )(
-        block_adapter,
+        block_adapter.reshape(nblk),
         block_count,
         features,
         upstream,
@@ -494,8 +483,7 @@
         adapter_down.reshape(ar, width),
         adapter_up.reshape(ar, outs),
     )
-    grad_up = gup.reshape(rank, tenants, oc).transpose(1, 0, 2)
-    return gin, gdn.reshape(tenants, rank, w), grad_up
+    return gin, gdn, gup
 
 
 def solution(mesh):

time: 44.7 us -> 36.3 us (0.81)
  local copies, waits for them, and re-layouts: 8.45 us -> 3.45 us
  Pallas kernels: 35.4 us -> 32.1 us
    unnamed x6 -> x7, local copies, waits for them, and re-layouts: 7.55 us -> 3.45 us
    pallas_call x1, Pallas kernels: 35.4 us -> 32.1 us  [per_device(): pl.pallas_call(functools.partial(kernel, dims), out_shape=(pltpu.VMEM((to...]
    reshape x1 -> x0, local copies, waits for them, and re-layouts: 0.9 us -> none  [per_device(): grad_up = gup.reshape(rank, tenants, oc).transpose(1, 0, 2)]
where the time goes in v2:
time: 36.3 us; the launch traced here: 36.2 us
  Pallas kernels  32.1 us (88%)
  local copies, waits for them, and re-layouts  3.45 us (10%)
  between operations  0.66 us (2%)
    pallas_call x1, Pallas kernels, per_device(): pl.pallas_call(functools.partial(kernel, dims), out_shape=(pltpu.VMEM((to...  32.1 us
    unnamed x7, local copies, waits for them, and re-layouts  3.45 us

profile of v2, /device:TPU:0, one launch (start us, length us, event | category | flops | bytes accessed | tf_op | source)
XLA Modules:
  0.0 36.2 jit_solution(15415819229168289617)
XLA Ops:
  0.6 32.1 %shard_map.94 = (bf16[512,4096]{1,0:T(8,128)(2,1)S(1)}, f32[12,32,256]{2,1,0:T(8,128)}, f32[12,32,32]{2,1,0:T(8,128)}) custom-call(s32[4]{0:T(128)} %bitcast.5, s32[4]{0:T(128)} %cnt_ref.1, bf16[512,4096]{1,0:T(8,128)(2,1)} %x_hbm.1, bf16[512,512]{1,0:T(8,128)(2,1)} %y_hbm.1, bf16[4096,512]{1,0:T(8,128)(2,1)} %fz_hbm.1, bf16[384,4096]{1,0:T(8,128)(2,1)} %bitcast.3, ...), custom_call_target="tpu_custom_call" | custom-call | flops 3758096384 | bytes 15728640 | tf_op jit(solution)/shard_map/pallas_call | solution.py:424
  32.7 0.0 copy-start
  32.7 0.0 copy-start.1
  32.7 2.0 %copy.13 = bf16[512,4096]{1,0:T(8,128)(2,1)} copy(bf16[512,4096]{1,0:T(8,128)(2,1)S(1)} %get-tuple-element.3) | data formatting | bytes 8388608
  34.7 0.0 copy-done
  34.7 0.7 %copy.14 = f32[12,32,256]{2,1,0:T(8,128)} copy(f32[12,32,256]{2,1,0:T(8,128)S(1)} %copy-done) | data formatting | bytes 786432
  35.5 0.0 copy-done.1
  35.5 0.7 %copy.15 = f32[12,32,32]{2,1,0:T(8,128)} copy(f32[12,32,32]{2,1,0:T(8,128)S(1)} %copy-done.1) | data formatting | bytes 98304
Async XLA Ops:
  32.7 2.0 %copy-start = (f32[12,32,256]{2,1,0:T(8,128)S(1)}, f32[12,32,256]{2,1,0:T(8,128)}, u32[]{:S(2)}) copy-start(f32[12,32,256]{2,1,0:T(8,128)} %get-tuple-element.10) | copy-start | bytes 1179652
  32.7 2.8 %copy-start.1 = (f32[12,32,32]{2,1,0:T(8,128)S(1)}, f32[12,32,32]{2,1,0:T(8,128)}, u32[]{:S(2)}) copy-start(f32[12,32,32]{2,1,0:T(8,128)} %get-tuple-element.11) | copy-start | bytes 147460

commit v3 on v2

--- a/solution.py
+++ b/solution.py
@@ -331,6 +331,9 @@
 
         ls[way, zc] = acc[...].astype(BF)
         line_copy(way, zc, False).start()
+
+    def up_hop(way, zc):
+        fed = z > 0 if way == 0 else z < outer - 1
         umerged(zc)
 
         @pl.when(fed)
@@ -351,6 +354,14 @@
         @pl.when(t >= outer - 1 - z)
         def _():
             hop(1, t - (outer - 1 - z))
+
+        @pl.when(t >= z)
+        def _():
+            up_hop(0, z + outer - 1 - t)
+
+        @pl.when(t >= outer - 1 - z)
+        def _():
+            up_hop(1, t - (outer - 1 - z))
 
         lo = first + (t * (tiles - first)) // (outer - 1)
         hi = first + ((t + 1) * (tiles - first)) // (outer - 1)

time: 36.3 us -> 35.8 us (0.986)
  Pallas kernels: 32.1 us -> 31.5 us
    pallas_call x1, Pallas kernels: 32.1 us -> 31.5 us  [per_device(): pl.pallas_call(functools.partial(kernel, dims), out_shape=(pltpu.VMEM((to...]
where the time goes in v3:
time: 35.8 us; the launch traced here: 35.6 us
  Pallas kernels  31.5 us (88%)
  local copies, waits for them, and re-layouts  3.45 us (10%)
  between operations  0.66 us (2%)
    pallas_call x1, Pallas kernels, per_device(): pl.pallas_call(functools.partial(kernel, dims), out_shape=(pltpu.VMEM((to...  31.5 us
    unnamed x7, local copies, waits for them, and re-layouts  3.45 us

profile of v3, /device:TPU:0, one launch (start us, length us, event | category | flops | bytes accessed | tf_op | source)
XLA Modules:
  0.0 35.6 jit_solution(2207901299367335819)
XLA Ops:
  0.6 31.5 %shard_map.94 = (bf16[512,4096]{1,0:T(8,128)(2,1)S(1)}, f32[12,32,256]{2,1,0:T(8,128)}, f32[12,32,32]{2,1,0:T(8,128)}) custom-call(s32[4]{0:T(128)} %bitcast.5, s32[4]{0:T(128)} %cnt_ref.1, bf16[512,4096]{1,0:T(8,128)(2,1)} %x_hbm.1, bf16[512,512]{1,0:T(8,128)(2,1)} %y_hbm.1, bf16[4096,512]{1,0:T(8,128)(2,1)} %fz_hbm.1, bf16[384,4096]{1,0:T(8,128)(2,1)} %bitcast.3, ...), custom_call_target="tpu_custom_call" | custom-call | flops 3758096384 | bytes 15728640 | tf_op jit(solution)/shard_map/pallas_call | solution.py:435
  32.1 0.0 copy-start
  32.2 0.0 copy-start.1
  32.2 2.0 %copy.13 = bf16[512,4096]{1,0:T(8,128)(2,1)} copy(bf16[512,4096]{1,0:T(8,128)(2,1)S(1)} %get-tuple-element.3) | data formatting | bytes 8388608
  34.2 0.0 copy-done
  34.2 0.7 %copy.14 = f32[12,32,256]{2,1,0:T(8,128)} copy(f32[12,32,256]{2,1,0:T(8,128)S(1)} %copy-done) | data formatting | bytes 786432
  34.9 0.0 copy-done.1
  34.9 0.7 %copy.15 = f32[12,32,32]{2,1,0:T(8,128)} copy(f32[12,32,32]{2,1,0:T(8,128)S(1)} %copy-done.1) | data formatting | bytes 98304
Async XLA Ops:
  32.1 2.0 %copy-start = (f32[12,32,256]{2,1,0:T(8,128)S(1)}, f32[12,32,256]{2,1,0:T(8,128)}, u32[]{:S(2)}) copy-start(f32[12,32,256]{2,1,0:T(8,128)} %get-tuple-element.10) | copy-start | bytes 1179652
  32.2 2.8 %copy-start.1 = (f32[12,32,32]{2,1,0:T(8,128)S(1)}, f32[12,32,32]{2,1,0:T(8,128)}, u32[]{:S(2)}) copy-start(f32[12,32,32]{2,1,0:T(8,128)} %get-tuple-element.11) | copy-start | bytes 147460
